TPU v7x, 32 devices: a whole 2x2x4 slice. The times are simulated.
32 devices in a mesh: dp: 4 (over z), tp: 8 (over y, x, core).
Axes of the slice: x: 2, y: 2, z: 4, core: 2. Of those that a mesh axis runs over, the one named last changes fastest.
Arguments:
- layer_input: bfloat16 [128, 7168], P(('dp', 'tp')), may hold values from -16 to 16
- query: bfloat16 [128, 64, 576], P(('dp', 'tp')), may hold values from -48 to 48
- cache: bfloat16 [128, 2048, 576], P(('dp', 'tp')), may hold values from -8 to 8
- lengths: int32 [128], P(('dp', 'tp')), may hold values from 2 to 2048, as said below
- counts: int32 [32], P(('dp', 'tp')), may hold values from 1 to 4, as said below
- value_weight: bfloat16 [64, 512, 128], P('tp'), may hold values from -0.25 to 0.25
- output_weight: bfloat16 [8192, 7168], P('tp'), may hold values from -0.0625 to 0.0625
- norm_gain: float32 [7168], replicated, may hold values from 0.1 to 1.9
- gate_weight: bfloat16 [7168, 9216], P(None, 'tp'), may hold values from -0.0625 to 0.0625
- up_weight: bfloat16 [7168, 9216], P(None, 'tp'), may hold values from -0.0625 to 0.0625
- down_weight: bfloat16 [9216, 7168], P('tp', 'dp'), may hold values from -0.0625 to 0.0625
Outputs:
- layer_output: bfloat16 [128, 7168], P(('dp', 'tp'))
Inputs may be any that keep to these rules, and one draw needn't show every extreme that they name: `counts`: one device holds 4 live slots and another one. `lengths`: on every device some live slot has 2048 valid positions.
All inputs are finite; a program needn't handle non-finite values.
Results may differ from a plain program's by a relative error of at most 0.014.
Values may be sent and summed in bfloat16 or wider, within the bound.
A program may use at most 128 MiB of HBM per device.

v0:
```python
import jax
import jax.numpy as jnp
from jax import lax
from jax.sharding import PartitionSpec as P

score_scale = 1.0 / 192.0**0.5
norm_eps = 1e-06


def normalize(residual, norm_gain):
    wide = residual.astype(jnp.float32)
    square_mean = jnp.mean(wide * wide, axis=1, keepdims=True)
    return (wide * lax.rsqrt(square_mean + norm_eps) * norm_gain[None, :]).astype(jnp.bfloat16)


def on_device(
    layer_input,
    query,
    cache,
    lengths,
    counts,
    value_weight,
    output_weight,
    norm_gain,
    gate_weight,
    up_weight,
    down_weight,
):
    slot_count = layer_input.shape[0]
    latent_width = value_weight.shape[1]
    positions = jnp.arange(cache.shape[1], dtype=jnp.int32)
    visible = positions[None, None, :] < lengths[:, None, None]
    scores = (
        jnp.einsum("rhc,rtc->rht", query, cache, preferred_element_type=jnp.float32) * score_scale
    )
    scores = jnp.where(visible, scores, jnp.float32(-1e30))
    peak = jnp.max(scores, axis=2, keepdims=True)
    raised = jnp.where(visible, jnp.exp(scores - peak), jnp.float32(0.0))
    attention = (raised / jnp.sum(raised, axis=2, keepdims=True)).astype(jnp.bfloat16)
    latent = jnp.einsum(
        "rht,rta->rha", attention, cache[:, :, :latent_width], preferred_element_type=jnp.float32
    ).astype(jnp.bfloat16)
    arrived = lax.all_to_all(latent, "tp", split_axis=1, concat_axis=0, tiled=True)
    values = jnp.einsum(
        "gha,had->ghd", arrived, value_weight, preferred_element_type=jnp.float32
    ).astype(jnp.bfloat16)
    flat = values.reshape(values.shape[0], values.shape[1] * values.shape[2])
    begin = lax.axis_index("tp") * slot_count
    attended = lax.psum(jnp.dot(flat, output_weight, preferred_element_type=jnp.float32), "tp")
    every_input = lax.all_gather(layer_input, "tp", axis=0, tiled=True)
    residual_group = (every_input.astype(jnp.float32) + attended).astype(jnp.bfloat16)
    normed_group = normalize(residual_group, norm_gain)
    residual = lax.dynamic_slice_in_dim(residual_group, begin, slot_count, 0)
    gate = jnp.dot(normed_group, gate_weight, preferred_element_type=jnp.float32)
    upward = jnp.dot(normed_group, up_weight, preferred_element_type=jnp.float32)
    inner = (jax.nn.silu(gate) * upward).astype(jnp.bfloat16)
    partial_value = jnp.dot(
        inner,
        lax.all_gather(down_weight, "dp", axis=1, tiled=True),
        preferred_element_type=jnp.float32,
    )
    feed = lax.psum_scatter(
        partial_value.astype(jnp.bfloat16), "tp", scatter_dimension=0, tiled=True
    ).astype(jnp.float32)
    mixed = residual.astype(jnp.float32) + feed
    live = jnp.arange(slot_count, dtype=jnp.int32) < counts[0]
    return jnp.where(live[:, None], mixed, jnp.float32(0.0)).astype(jnp.bfloat16)


def solution(mesh):
    placed = (
        P(("dp", "tp"), None),
        P(("dp", "tp"), None, None),
        P(("dp", "tp"), None, None),
        P(("dp", "tp")),
        P(("dp", "tp")),
        P("tp", None, None),
        P("tp", None),
        P(),
        P(None, "tp"),
        P(None, "tp"),
        P("tp", "dp"),
    )
    return jax.shard_map(
        on_device, mesh=mesh, in_specs=placed, out_specs=P(("dp", "tp"), None), check_vma=False
    )
```

profile of v0, /device:TPU:0, one launch (start us, length us, event | category | flops | bytes accessed | tf_op | source)
XLA Modules:
  0.0 404.5 jit_solution(5665862228317510705)
XLA Ops:
  7.4 0.8 iota_compare_fusion
  8.2 6.2 %fusion.30 = (f32[4,64]{1,0:T(4,128)S(1)}, f32[4,64,2048]{2,1,0:T(8,128)S(1)}) fusion(pred[4,2048]{1,0:T(4,128)(4,1)S(1)} %iota_compare_fusion, bf16[4,64,576]{2,1,0:T(8,128)(2,1)} %param.12, bf16[4,2048,576]{1,2,0:T(8,128)(2,1)} %param.13), kind=kOutput, calls=%fused_computation.38 | convolution fusion | flops 606603264 | bytes 11838464 | tf_op jit(solution)/shard_map/sub | solution.py:38
  14.4 6.1 %fusion.8 = bf16[4,64,512]{2,1,0:T(8,128)(2,1)S(1)} fusion(bf16[4,2048,576]{1,2,0:T(8,128)(2,1)} %param.13, f32[4,64,2048]{2,1,0:T(8,128)S(1)} %get-tuple-element.8, f32[4,64]{1,0:T(4,128)S(1)} %get-tuple-element.7), kind=kOutput, calls=%fused_computation.12 | convolution fusion | flops 538050560 | bytes 10748928 | tf_op jit(solution)/shard_map/rht,rta->rha/dot_general | solution.py:40
  20.5 0.2 copy.18
  20.7 11.9 %all_to_all.18 = bf16[4,64,512]{2,0,1:T(4,128)(2,1)S(1)} all-to-all(bf16[4,64,512]{2,0,1:T(4,128)(2,1)S(1)} %copy.18), channel_id=1, replica_groups=mesh['dp'=4,'tp'=8] {'tp'}, dimensions={1} | all-to-all | bytes 524288 | tf_op jit(solution)/shard_map/all_to_all | solution.py:43
  32.6 0.1 copy.28
  32.7 0.1 all_to_all.16
  32.8 0.3 fusion.11
  33.1 8.8 %fusion.26 = f32[32,7168]{1,0:T(8,128)} fusion(bf16[1024,7168]{1,0:T(8,128)(2,1)} %param.17, bf16[8,4,8,128]{3,2,1,0:T(8,128)(2,1)S(1)} %fusion.11), kind=kOutput, calls=%fused_computation.31 | convolution fusion | flops 469762048 | bytes 15663104 | tf_op jit(solution)/shard_map/dot_general | solution.py:49
  41.9 0.0 all-reduce.4.cloned.1.call-update
  41.9 0.0 all-gather.3.cloned.1.call-start
  41.9 0.5 all-gather.3.cloned.1.call-update
  42.5 0.0 all-reduce.6.cloned.1.call-start
  42.5 9.2 %all-gather = bf16[8,4,7168]{2,1,0:T(4,128)(2,1)S(1)} all-gather(bf16[1,4,7168]{2,1,0:T(4,128)(2,1)S(1)} %bitcast.26), channel_id=1, replica_groups=mesh['dp'=4,'tp'=8] {'tp'}, dimensions={0}, use_global_device_ids=true | all-gather | bytes 516096 | tf_op jit(solution)/shard_map/all_gather | solution.py:50
  51.7 0.1 reshape.42
  51.8 45.9 %all-reduce.4.cloned.1.call-done = f32[32,7168]{1,0:T(8,128)} async-done(((f32[32,7168]{1,0:T(8,128)}), f32[32,7168]{1,0:T(8,128)}) %all-reduce.4.cloned.1.call-update) | async-done | bytes 917520 | tf_op jit(solution)/shard_map/psum | solution.py:49
  97.6 1.4 fusion.13
  99.0 8.7 %fusion.23 = f32[32,1152]{1,0:T(8,128)S(1)} fusion(bf16[7168,1152]{1,0:T(8,128)(2,1)} %param.19, bf16[32,7168]{1,0:T(8,128)(2,1)S(1)} %get-tuple-element.6, f32[7168]{0:T(1024)S(1)} %copy-done.2, f32[32]{0:T(128)S(1)} %add_rsqrt_fusion), kind=kOutput, calls=%fused_computation.28 | convolution fusion | flops 529399808 | bytes 17150080 | tf_op jit(solution)/shard_map/dot_general | solution.py:54
  107.8 217.9 %all-gather.3.cloned.1.call-done = bf16[1152,7168]{1,0:T(8,128)(2,1)} async-done(((bf16[1152,1792]{1,0:T(8,128)(2,1)}), bf16[1152,7168]{1,0:T(8,128)(2,1)}) %all-gather.3.cloned.1.call-update) | async-done | bytes 16515088 | tf_op jit(solution)/shard_map/all_gather | solution.py:59
  325.7 17.0 %convolution_convert_fusion = bf16[32,7168]{1,0:T(8,128)(2,1)} fusion(bf16[1152,7168]{1,0:T(8,128)(2,1)} %all-gather.3.cloned.1.call-done, bf16[7168,1152]{1,0:T(8,128)(2,1)} %param.20, f32[32,1152]{1,0:T(8,128)S(1)} %fusion.23, bf16[32,7168]{1,0:T(8,128)(2,1)S(1)} %get-tuple-element.6, f32[7168]{0:T(1024)S(1)} %copy-done.2, f32[32]{0:T(128)S(1)} %add_rsqrt_fusion), kind=kOutput, calls=%fused_computation.3 | convolution fusion | flops 1058332672 | bytes 34123904 | tf_op jit(solution)/shard_map/dot_general | solution.py:57
  342.7 0.0 all-reduce.6.cloned.1.call-update
  343.4 0.6 dynamic-slice
  344.6 50.8 %all-reduce.6.cloned.1.call-done = bf16[32,7168]{1,0:T(8,128)(2,1)} async-done(((bf16[32,7168]{1,0:T(8,128)(2,1)}), bf16[32,7168]{1,0:T(8,128)(2,1)}) %all-reduce.6.cloned.1.call-update) | async-done | bytes 458768
  395.4 1.6 select_convert_fusion
  (13 shorter events, 0.0 us)
Async XLA Ops:
  7.4 25.4 %copy-start = (bf16[8,512,128]{2,1,0:T(8,128)(2,1)S(1)}, bf16[8,512,128]{2,1,0:T(8,128)(2,1)}, u32[]{:S(2)}) copy-start(bf16[8,512,128]{2,1,0:T(8,128)(2,1)} %param.16) | copy-start | bytes 3145732
  7.4 90.3 %all-reduce.4.cloned.1.call-start = ((), (), s32[]{:S(2)}) async-start(), calls=%async_computation.1 | async-start | bytes 1835008 | tf_op jit(solution)/shard_map/psum | solution.py:49
  33.0 9.5 %copy-start.3 = (bf16[4,7168]{1,0:T(4,128)(2,1)S(1)}, bf16[4,7168]{1,0:T(4,128)(2,1)}, u32[]{:S(2)}) copy-start(bf16[4,7168]{1,0:T(4,128)(2,1)} %param.11) | copy-start | bytes 172036
  33.0 66.0 %copy-start.2 = (f32[7168]{0:T(1024)S(1)}, f32[7168]{0:T(1024)}, u32[]{:S(2)}) copy-start(f32[7168]{0:T(1024)} %param.18) | copy-start | bytes 86020
  41.9 283.8 %all-gather.3.cloned.1.call-start = ((), (), s32[]{:S(2)}) async-start(), calls=%async_computation.2 | async-start | bytes 20643840 | tf_op jit(solution)/shard_map/all_gather | solution.py:59
  42.5 353.0 %all-reduce.6.cloned.1.call-start = ((), (), s32[]{:S(2)}) async-start(), calls=%async_computation.3 | async-start | bytes 917504
  99.0 298.0 %copy-start.1 = (bf16[8,512,128]{2,1,0:T(8,128)(2,1)S(1)}, bf16[8,512,128]{2,1,0:T(8,128)(2,1)}, u32[]{:S(2)}) copy-start(bf16[8,512,128]{2,1,0:T(8,128)(2,1)} %param.16) | copy-start | bytes 3145732
  107.8 235.6 %copy-start.4 = (u32[32]{0:T(128)S(1)}, u32[32]{0:T(128)}, u32[]{:S(2)}) copy-start(u32[32]{0:T(128)} %constant.33) | copy-start | bytes 388
Sparse Core Ops, SparseCore 0:
  42.0 55.5 all-reduce.3
  342.8 52.5 all-reduce.5
Sparse Core Ops, SparseCore 1:
  43.9 281.7 all-gather.2
where the time goes:
time: 405 us; the launch traced here: 404 us
  waiting for transfers between devices  315 us (78%)
  matrix products  47.1 us (12%)
  blocking collectives  21.1 us (5%)
  between operations  16.3 us (4%)
    all_gather x1, waiting for transfers between devices, on_device(): lax.all_gather(down_weight, 'dp', axis=1, tiled=True)  218 us
    unnamed x4, waiting for transfers between devices  51.4 us
    psum x1, waiting for transfers between devices, on_device(): lax.psum(jnp.dot(flat, output_weight, preferred_element_type=jnp.float32)...  45.9 us
    dot_general x1, matrix products, on_device(): jnp.dot(inner, lax.all_gather(down_weight, 'dp', axis=1, tiled=True), pre...  17 us
    all_to_all x1, blocking collectives, on_device(): lax.all_to_all(latent, 'tp', split_axis=1, concat_axis=0, tiled=True)  11.9 us
    all_gather x1, blocking collectives, on_device(): every_input = lax.all_gather(layer_input, 'tp', axis=0, tiled=True)  9.16 us
    dot_general x1, matrix products, on_device(): jnp.dot(flat, output_weight, preferred_element_type=jnp.float32)  8.81 us
    dot_general x1, matrix products, on_device(): jnp.dot(normed_group, gate_weight, preferred_element_type=jnp.float32)  8.72 us
  transfers between devices with their start and end apart: 3, of which 3 were waited for; matrix products, arithmetic and copies ran while one was open for 3% of the time, Pallas kernels for 0%

commit v1 on v0

v1 whole, which is shorter than its diff:
```python
import functools
import math

import jax
import jax.numpy as jnp
import numpy as np
from jax import lax
from jax.experimental import pallas as pl
from jax.experimental.pallas import tpu as pltpu
from jax.sharding import PartitionSpec as P

score_scale = 1.0 / 192.0**0.5
norm_eps = 1e-06
MESH = pl.DeviceIdType.MESH
F32 = jnp.float32
BF16 = jnp.bfloat16


def row_moves(n, m, slots, heads):
    each = heads // n
    send = np.zeros((slots * heads, slots * heads), np.float32)
    for o in range(slots * heads):
        j, r, h = o // (slots * each), (o // each) % slots, o % each
        send[o, r * heads + j * each + h] = 1
    group = n * slots
    take = np.zeros((each * group, each * group), np.float32)
    for o in range(each * group):
        h, j, r = o // group, (o % group) // slots, o % slots
        take[o, (j * slots + r) * each + h] = 1
    turn = np.zeros((m * group, m * group), np.float32)
    for o in range(m * group):
        j, g, r = o // (m * slots), (o // slots) % m, o % slots
        turn[o, g * group + j * slots + r] = 1
    return [x.astype(jnp.bfloat16) for x in (send, take, turn)]


def kernel(
    n,
    m,
    blocks,
    lengths,
    counts,
    layer_input,
    query,
    cache,
    value_weight,
    output_weight,
    gain,
    gate_weight,
    up_weight,
    down_weight,
    send_move,
    take_move,
    turn_move,
    out,
    cache_v,
    value_v,
    wo_v,
    gate_v,
    up_v,
    down_v,
    lat,
    lat_send,
    lat_recv,
    flat,
    rs_send,
    rs_recv,
    rs_own,
    ag,
    acc_gate,
    acc_up,
    square,
    inner,
    fs_send,
    fs_recv,
    z_send,
    z_recv,
    cache_sem,
    one_sem,
    wo_sem,
    gate_sem,
    up_sem,
    send_sem,
    recv_sem,
    dp_send_sem,
    dp_recv_sem,
):
    i = lax.axis_index("dp")
    j = lax.axis_index("tp")
    slots, heads, _ = query.shape
    width = lat.shape[2]
    group = n * slots
    rows = rs_send.shape[1]
    cols = rs_send.shape[2]
    each = heads // n
    row_blocks = group // rows
    jf = lax.rem(j, blocks)
    jr = lax.div(j, blocks)

    def cache_copy(r):
        slot = lax.rem(r, 2)
        return pltpu.make_async_copy(cache.at[r], cache_v.at[slot], cache_sem.at[slot])

    def wo_copy(b):
        source = output_weight.at[:, pl.ds(pl.multiple_of(b * cols, 128), cols)]
        return pltpu.make_async_copy(source, wo_v.at[b], wo_sem.at[b])

    def gate_copy(b):
        source = gate_weight.at[pl.ds(pl.multiple_of(b * cols, 128), cols), :]
        return pltpu.make_async_copy(source, gate_v.at[b], gate_sem.at[b])

    def up_copy(b):
        source = up_weight.at[pl.ds(pl.multiple_of(b * cols, 128), cols), :]
        return pltpu.make_async_copy(source, up_v.at[b], up_sem.at[b])

    value_copy = pltpu.make_async_copy(value_weight, value_v, one_sem.at[0])
    down_copy = pltpu.make_async_copy(down_weight, down_v, one_sem.at[1])

    def tp_copy(phase, source, target, peer, mine):
        return pltpu.make_async_remote_copy(
            src_ref=source,
            dst_ref=target,
            send_sem=send_sem.at[phase, peer],
            recv_sem=recv_sem.at[phase, mine],
            device_id=(i, peer),
            device_id_type=MESH,
        )

    def dp_copy(phase, source, target, peer, mine):
        return pltpu.make_async_remote_copy(
            src_ref=source,
            dst_ref=target,
            send_sem=dp_send_sem.at[phase, peer],
            recv_sem=dp_recv_sem.at[phase, mine],
            device_id=(peer, j),
            device_id_type=MESH,
        )

    def loop(count, body, first=0):
        def step(t, carry):
            body(t)
            return carry

        lax.fori_loop(first, count, step, 0)

    cache_copy(0).start()
    cache_copy(1).start()
    value_copy.start()
    loop(blocks, lambda t: wo_copy(lax.rem(jf + 1 + t, blocks)).start())

    barrier = pltpu.get_barrier_semaphore()

    def greet_tp(d):
        pl.semaphore_signal(
            barrier, inc=1, device_id=(i, lax.rem(j + d, n)), device_id_type=MESH
        )

    def greet_dp(d):
        pl.semaphore_signal(
            barrier, inc=1, device_id=(lax.rem(i + d, m), j), device_id_type=MESH
        )

    loop(n, greet_tp, 1)
    loop(m, greet_dp, 1)

    def attend(r):
        slot = lax.rem(r, 2)
        cache_copy(r).wait()
        question = query[r]
        stored = cache_v[slot]
        scores = (
            lax.dot_general(
                question, stored, (((1,), (1,)), ((), ())), preferred_element_type=F32
            )
            * score_scale
        )
        visible = lax.broadcasted_iota(jnp.int32, scores.shape, 1) < lengths[r]
        scores = jnp.where(visible, scores, F32(-1e30))
        peak = jnp.max(scores, axis=1, keepdims=True)
        raised = jnp.where(visible, jnp.exp(scores - peak), F32(0.0))
        total = jnp.sum(raised, axis=1, keepdims=True)
        mixed = jnp.dot(raised.astype(BF16), stored[:, :width], preferred_element_type=F32)
        lat[r] = (mixed / total).astype(BF16)

        @pl.when(r + 2 < slots)
        def _():
            cache_copy(r + 2).start()

        @pl.when(r == 1)
        def _():
            loop(blocks, lambda b: gate_copy(b).start())
            loop(blocks, lambda b: up_copy(b).start())
            down_copy.start()

    loop(slots, attend)

    moved = jnp.dot(
        send_move[...], lat[...].reshape(slots * heads, width), preferred_element_type=F32
    )
    lat_send[...] = moved.reshape(n, slots * each, width).astype(BF16)
    pl.semaphore_wait(barrier, n - 1 + m - 1)

    def send_latent(d):
        peer = lax.rem(j + d, n)
        tp_copy(0, lat_send.at[peer], lat_recv.at[j], peer, j).start()

    loop(n, send_latent, 1)
    lat_recv[j] = lat_send[j]
    value_copy.wait()

    def wait_latent(d):
        peer = lax.rem(j + n - d, n)
        tp_copy(0, lat_send.at[peer], lat_recv.at[peer], peer, peer).wait_recv()

    loop(n, wait_latent, 1)

    arrived = lat_recv[...].astype(F32).reshape(group * each, width).astype(BF16)
    taken = jnp.dot(take_move[...], arrived, preferred_element_type=F32).astype(BF16)
    head = value_v.shape[2]
    for h in range(each):
        flat[:, h * head : (h + 1) * head] = jnp.dot(
            taken[h * group : (h + 1) * group], value_v[h], preferred_element_type=F32
        ).astype(BF16)

    def project(t):
        b = lax.rem(jf + 1 + t, blocks)
        wo_copy(b).wait()
        part = jnp.dot(flat[...], wo_v[b], preferred_element_type=F32)
        mine = layer_input[:, pl.ds(pl.multiple_of(b * cols, 128), cols)].astype(F32)
        row = lax.broadcasted_iota(jnp.int32, part.shape, 0)
        for r in range(slots):
            part = part + jnp.where(row == j * slots + r, mine[r : r + 1, :], F32(0.0))
        for k in range(row_blocks):
            peer = k * blocks + b
            piece = part[k * rows : (k + 1) * rows]

            @pl.when(peer == j)
            def _():
                rs_own[...] = piece

            @pl.when(peer != j)
            def _():
                rs_send[peer] = piece.astype(BF16)
                tp_copy(1, rs_send.at[peer], rs_recv.at[j], peer, j).start()

    loop(blocks, project)

    def add_part(d):
        peer = lax.rem(j + n - d, n)
        tp_copy(1, rs_send.at[peer], rs_recv.at[peer], peer, peer).wait_recv()
        rs_own[...] += rs_recv[peer].astype(F32)

    loop(n, add_part, 1)
    ag[j] = rs_own[...].astype(BF16)

    def send_residual(d):
        peer = lax.rem(j + d, n)
        tp_copy(2, ag.at[j], ag.at[j], peer, j).start()

    loop(n, send_residual, 1)
    acc_gate[...] = jnp.zeros_like(acc_gate)
    acc_up[...] = jnp.zeros_like(acc_up)
    square[...] = jnp.zeros_like(square)

    def wait_weights(b):
        gate_copy(b).wait()
        up_copy(b).wait()

    loop(blocks, wait_weights)

    def expand(d):
        peer = lax.rem(j + n - d, n)

        @pl.when(d > 0)
        def _():
            tp_copy(2, ag.at[peer], ag.at[peer], peer, peer).wait_recv()

        k = lax.div(peer, blocks)
        b = lax.rem(peer, blocks)
        wide = ag[peer].astype(F32)
        square[k] += jnp.sum(wide * wide, axis=1, keepdims=True)
        scaled = (wide * gain[b]).astype(BF16)
        acc_gate[k] += jnp.dot(scaled, gate_v[b], preferred_element_type=F32)
        acc_up[k] += jnp.dot(scaled, up_v[b], preferred_element_type=F32)

    loop(n, expand)

    for k in range(row_blocks):
        norm = lax.rsqrt(square[k] * (1.0 / (blocks * cols)) + norm_eps)
        gate = acc_gate[k] * norm
        upward = acc_up[k] * norm
        inner[i, k * rows : (k + 1) * rows, :] = (
            gate / (1.0 + jnp.exp(-gate)) * upward
        ).astype(BF16)

    def send_inner(d):
        peer = lax.rem(i + d, m)
        dp_copy(0, inner.at[i], inner.at[i], peer, i).start()

    def wait_inner(d):
        peer = lax.rem(i + m - d, m)
        dp_copy(0, inner.at[peer], inner.at[peer], peer, peer).wait_recv()

    loop(m, send_inner, 1)
    down_copy.wait()
    loop(m, wait_inner, 1)

    every = inner[...].reshape(m * group, inner.shape[2])
    turned = jnp.dot(turn_move[...], every, preferred_element_type=F32).astype(BF16)
    fed = jnp.dot(turned, down_v[...], preferred_element_type=F32)
    fs_send[...] = fed.reshape(n, m * slots, fed.shape[1]).astype(BF16)

    def send_feed(d):
        peer = lax.rem(j + d, n)
        tp_copy(3, fs_send.at[peer], fs_recv.at[j], peer, j).start()

    loop(n, send_feed, 1)

    def add_feed(d, total):
        peer = lax.rem(j + n - d, n)
        tp_copy(3, fs_send.at[peer], fs_recv.at[peer], peer, peer).wait_recv()
        return total + fs_recv[peer].astype(F32)

    total = lax.fori_loop(1, n, add_feed, fs_send[j].astype(F32))
    pieces = blocks // m
    for g in range(m):
        for c in range(pieces):
            z_send[g, c * slots : (c + 1) * slots, :] = total[
                g * slots : (g + 1) * slots, c * cols : (c + 1) * cols
            ]

    def send_z(d):
        peer = lax.rem(i + d, m)
        dp_copy(1, z_send.at[peer], z_recv.at[i], peer, i).start()

    def wait_z(d):
        peer = lax.rem(i + m - d, m)
        dp_copy(1, z_send.at[peer], z_recv.at[peer], peer, peer).wait_recv()

    loop(m, send_z, 1)
    z_recv[i] = z_send[i]
    pick_row = lax.broadcasted_iota(jnp.int32, (8, rows), 0)
    pick_col = lax.broadcasted_iota(jnp.int32, (8, rows), 1)
    pick = jnp.where(pick_col == pick_row + jf * slots, F32(1.0), F32(0.0)).astype(BF16)
    live = lax.broadcasted_iota(jnp.int32, (slots, cols), 0) < counts[0]
    residual = [
        jnp.dot(pick, ag[jr * blocks + b], preferred_element_type=F32)[:slots]
        for b in range(blocks)
    ]
    loop(m, wait_z, 1)
    for b in range(blocks):
        g, c = b // pieces, b % pieces
        mixed = residual[b] + z_recv[g, c * slots : (c + 1) * slots, :]
        out[:, b * cols : (b + 1) * cols] = jnp.where(live, mixed, F32(0.0)).astype(BF16)

    def drain(d):
        peer = lax.rem(j + d, n)
        tp_copy(0, lat_send.at[peer], lat_recv.at[peer], peer, peer).wait_send()
        tp_copy(1, rs_send.at[peer], rs_recv.at[peer], peer, peer).wait_send()
        tp_copy(2, ag.at[j], ag.at[peer], peer, peer).wait_send()
        tp_copy(3, fs_send.at[peer], fs_recv.at[peer], peer, peer).wait_send()

    def drain_dp(d):
        peer = lax.rem(i + d, m)
        dp_copy(0, inner.at[i], inner.at[peer], peer, peer).wait_send()
        dp_copy(1, z_send.at[peer], z_recv.at[peer], peer, peer).wait_send()

    loop(n, drain, 1)
    loop(m, drain_dp, 1)


def on_device(
    n,
    m,
    layer_input,
    query,
    cache,
    lengths,
    counts,
    value_weight,
    output_weight,
    norm_gain,
    gate_weight,
    up_weight,
    down_weight,
):
    slots, features = layer_input.shape
    heads = query.shape[1]
    each, width, head = value_weight.shape
    hidden = gate_weight.shape[1]
    group = n * slots
    blocks = math.gcd(n, features // 128)
    cols = features // blocks
    rows = group * blocks // n
    part = down_weight.shape[1]
    moves = row_moves(n, m, slots, heads)
    vmem = pl.BlockSpec(memory_space=pltpu.VMEM)
    smem = pl.BlockSpec(memory_space=pltpu.SMEM)
    hbm = pl.BlockSpec(memory_space=pl.ANY)
    dma = pltpu.SemaphoreType.DMA
    return pl.pallas_call(
        functools.partial(kernel, n, m, blocks),
        out_shape=jax.ShapeDtypeStruct((slots, features), BF16),
        in_specs=[smem, smem, vmem, vmem, hbm, hbm, hbm, vmem, hbm, hbm, hbm, vmem, vmem, vmem],
        out_specs=vmem,
        scratch_shapes=[
            pltpu.VMEM((2,) + cache.shape[1:], BF16),
            pltpu.VMEM(value_weight.shape, BF16),
            pltpu.VMEM((blocks, each * head, cols), BF16),
            pltpu.VMEM((blocks, cols, hidden), BF16),
            pltpu.VMEM((blocks, cols, hidden), BF16),
            pltpu.VMEM(down_weight.shape, BF16),
            pltpu.VMEM((slots, heads, width), BF16),
            pltpu.VMEM((n, slots * each, width), BF16),
            pltpu.VMEM((n, slots * each, width), BF16),
            pltpu.VMEM((group, each * head), BF16),
            pltpu.VMEM((n, rows, cols), BF16),
            pltpu.VMEM((n, rows, cols), BF16),
            pltpu.VMEM((rows, cols), F32),
            pltpu.VMEM((n, rows, cols), BF16),
            pltpu.VMEM((group // rows, rows, hidden), F32),
            pltpu.VMEM((group // rows, rows, hidden), F32),
            pltpu.VMEM((group // rows, rows, 1), F32),
            pltpu.VMEM((m, group, hidden), BF16),
            pltpu.VMEM((n, m * slots, part), BF16),
            pltpu.VMEM((n, m * slots, part), BF16),
            pltpu.VMEM((m, slots * blocks // m, cols), F32),
            pltpu.VMEM((m, slots * blocks // m, cols), F32),
            dma((2,)),
            dma((2,)),
            dma((blocks,)),
            dma((blocks,)),
            dma((blocks,)),
            dma((4, n)),
            dma((4, n)),
            dma((2, m)),
            dma((2, m)),
        ],
        compiler_params=pltpu.CompilerParams(
            collective_id=0, has_side_effects=True, vmem_limit_bytes=64 * 1024 * 1024
        ),
    )(
        lengths,
        counts,
        layer_input,
        query,
        cache,
        value_weight,
        output_weight,
        norm_gain.reshape(blocks, 1, cols),
        gate_weight,
        up_weight,
        down_weight,
        *[jnp.asarray(x) for x in moves],
    )


def solution(mesh):
    placed = (
        P(("dp", "tp"), None),
        P(("dp", "tp"), None, None),
        P(("dp", "tp"), None, None),
        P(("dp", "tp")),
        P(("dp", "tp")),
        P("tp", None, None),
        P("tp", None),
        P(),
        P(None, "tp"),
        P(None, "tp"),
        P("tp", "dp"),
    )
    return jax.shard_map(
        functools.partial(on_device, mesh.shape["tp"], mesh.shape["dp"]),
        mesh=mesh,
        in_specs=placed,
        out_specs=P(("dp", "tp"), None),
        check_vma=False,
    )
```

time: 405 us -> 75.6 us (0.19)
  waiting for transfers between devices: 315 us -> 0 us
  Pallas kernels: 0 us -> 58.8 us
  matrix products: 47.1 us -> 0 us
  blocking collectives: 21.1 us -> 0 us
  between operations: 16.3 us -> 0.66 us
  local copies, waits for them, and re-layouts: 1.04 us -> 15.6 us
    all_gather x1 -> x0, waiting for transfers between devices: 218 us -> none  [on_device(): lax.all_gather(down_weight, 'dp', axis=1, tiled=True)]
    pallas_call x0 -> x1, Pallas kernels: none -> 58.8 us  [on_device(): pl.pallas_call(functools.partial(kernel, n, m, blocks), out_shape=jax.Sha...]
    unnamed x4 -> x0, waiting for transfers between devices: 51.4 us -> none
    psum x1 -> x0, waiting for transfers between devices: 45.9 us -> none  [on_device(): lax.psum(jnp.dot(flat, output_weight, preferred_element_type=jnp.float32)...]
    dot_general x5 -> x0, matrix products: 40.9 us -> none  [the longest x1 17 us: on_device(): jnp.dot(inner, lax.all_gather(down_weight, 'dp', axis=1, tiled=True), pre...]
    unnamed x11 -> x2, local copies, waits for them, and re-layouts: 0.62 us -> 15.6 us
    all_to_all x1 -> x0, blocking collectives: 11.9 us -> none  [on_device(): lax.all_to_all(latent, 'tp', split_axis=1, concat_axis=0, tiled=True)]
    all_gather x1 -> x0, blocking collectives: 9.16 us -> none  [on_device(): every_input = lax.all_gather(layer_input, 'tp', axis=0, tiled=True)]
  transfers between devices with their start and end apart: 3 -> 0, of which waited for: 3 -> 0; matrix products, arithmetic and copies ran while one was open for 3% -> 0% of each run, Pallas kernels for 0% -> 0%
where the time goes in v1:
time: 75.6 us; the launch traced here: 75.1 us
  Pallas kernels  58.8 us (78%)
  local copies, waits for them, and re-layouts  15.6 us (21%)
    pallas_call x1, Pallas kernels, on_device(): pl.pallas_call(functools.partial(kernel, n, m, blocks), out_shape=jax.Sha...  58.8 us
    unnamed x2, local copies, waits for them, and re-layouts  15.6 us

profile of v1, /device:TPU:0, one launch (start us, length us, event | category | flops | bytes accessed | tf_op | source)
XLA Modules:
  0.0 75.1 jit_solution(3849592414831039803)
XLA Ops:
  0.7 14.2 %copy.15.cache = bf16[4,2048,576]{2,1,0:T(8,128)(2,1)} copy(bf16[4,2048,576]{1,2,0:T(8,128)(2,1)} %param.16) | data formatting | bytes 18874368 | tf_op args[2]
  14.8 58.8 %shard_map.136 = bf16[4,7168]{1,0:T(4,128)(2,1)} custom-call(s32[4]{0:T(128)} %lengths.1, s32[1]{0:T(128)S(6)} %copy.17.counts, bf16[4,7168]{1,0:T(4,128)(2,1)} %layer_input.1, bf16[4,64,576]{2,1,0:T(8,128)(2,1)} %query.1, bf16[4,2048,576]{2,1,0:T(8,128)(2,1)} %copy.15.cache, bf16[8,512,128]{2,1,0:T(8,128)(2,1)} %value_weight.1, ...), custom_call_target="tpu_custom_call" | custom-call | tf_op jit(solution)/shard_map/pallas_call | solution.py:401
  73.6 1.5 %copy.18 = bf16[4,7168]{1,0:T(4,128)(2,1)} copy(bf16[4,7168]{1,0:T(4,128)(2,1)} %shard_map.136) | data formatting | bytes 114688

commit v2 on v1

v2 whole, which is shorter than its diff:
```python
import functools
import math

import jax
import jax.numpy as jnp
import numpy as np
from jax import lax
from jax.experimental import pallas as pl
from jax.experimental.pallas import tpu as pltpu
from jax.sharding import PartitionSpec as P

score_scale = 1.0 / 192.0**0.5
norm_eps = 1e-06
MESH = pl.DeviceIdType.MESH
F32 = jnp.float32
BF16 = jnp.bfloat16


def row_moves(n, m, slots, heads):
    each, half = heads // n, slots // 2
    group = n * slots
    send = np.zeros((half * heads, half * heads), np.float32)
    for o in range(half * heads):
        j, r, h = o // (half * each), (o // each) % half, o % each
        send[o, r * heads + j * each + h] = 1
    take = np.zeros((2, each * group, half * heads), np.float32)
    for o in range(each * group):
        h, j, r = o // group, (o % group) // slots, o % slots
        take[r // half, o, (j * half + r % half) * each + h] = 1
    turn = np.zeros((m * group, m * group), np.float32)
    for o in range(m * group):
        j, g, r = o // (m * slots), (o // slots) % m, o % slots
        turn[o, g * group + j * slots + r] = 1
    return [x.astype(jnp.bfloat16) for x in (send, take, turn)]


def hidden_parts(hidden):
    if hidden % 128 or hidden < 512:
        return ((0, hidden),)
    first = (hidden // 2 + 127) // 128 * 128
    return ((0, first), (first, hidden))


def hidden_chunks(hidden):
    return tuple(
        tuple((at, min(at + 512, hi)) for at in range(lo, hi, 512)) for lo, hi in hidden_parts(hidden)
    )


def kernel(
    n,
    m,
    blocks,
    lengths,
    counts,
    layer_input,
    query,
    cache,
    value_weight,
    output_weight,
    gain,
    gate_weight,
    up_weight,
    down_weight,
    send_move,
    take_move,
    turn_move,
    out,
    cache_v,
    value_v,
    wo_v,
    gate_v,
    up_v,
    lat,
    lat_send,
    lat_recv,
    flat,
    rs_send,
    rs_recv,
    rs_own,
    ag,
    acc_gate,
    acc_up,
    square,
    inner,
    fs_recv,
    z_wide,
    z_send,
    z_recv,
    cache_sem,
    one_sem,
    wo_sem,
    gate_sem,
    up_sem,
    send_sem,
    recv_sem,
    dp_send_sem,
    dp_recv_sem,
):
    i = lax.axis_index("dp")
    j = lax.axis_index("tp")
    slots, heads, _ = query.shape
    half = slots // 2
    width = lat.shape[2]
    group = n * slots
    rows = rs_send.shape[1]
    cols = rs_send.shape[2]
    each = heads // n
    row_blocks = group // rows
    chips = n // 2
    pairs = blocks // 2
    wide_cols = 2 * cols
    parts = hidden_parts(gate_weight.shape[1])
    jf = lax.rem(j, blocks)
    jr = lax.div(j, blocks)
    core = lax.rem(j, 2)
    chip = lax.div(j, 2)
    sibling = chip * 2 + 1 - core
    ring = cache_v.shape[0]

    def cache_copy(r):
        slot = r % ring
        return pltpu.make_async_copy(cache.at[r], cache_v.at[slot], cache_sem.at[slot])

    def wo_copy(b):
        source = output_weight.at[:, pl.ds(pl.multiple_of(b * wide_cols, 128), wide_cols)]
        return pltpu.make_async_copy(source, wo_v.at[b], wo_sem.at[b])

    def gate_copy(b):
        source = gate_weight.at[pl.ds(pl.multiple_of(b * wide_cols, 128), wide_cols), :]
        return pltpu.make_async_copy(source, gate_v.at[b], gate_sem.at[b])

    def up_copy(b):
        source = up_weight.at[pl.ds(pl.multiple_of(b * wide_cols, 128), wide_cols), :]
        return pltpu.make_async_copy(source, up_v.at[b], up_sem.at[b])

    value_copy = pltpu.make_async_copy(value_weight, value_v, one_sem.at[0])
    chunks = hidden_chunks(gate_weight.shape[1])
    features = down_weight.shape[1]
    places = {c: k for k, c in enumerate(c for chunk in chunks for c in chunk)}

    def down_view(chunk):
        return cache_v.at[places[chunk], pl.ds(0, chunk[1] - chunk[0]), pl.ds(0, features)]

    def down_copy(chunk):
        source = down_weight.at[pl.ds(chunk[0], chunk[1] - chunk[0]), :]
        return pltpu.make_async_copy(source, down_view(chunk), one_sem.at[1 + places[chunk]])


    def tp_copy(phase, source, target, peer, mine):
        return pltpu.make_async_remote_copy(
            src_ref=source,
            dst_ref=target,
            send_sem=send_sem.at[phase, peer],
            recv_sem=recv_sem.at[phase, mine],
            device_id=(i, peer),
            device_id_type=MESH,
        )

    def dp_copy(phase, source, target, peer, mine):
        return pltpu.make_async_remote_copy(
            src_ref=source,
            dst_ref=target,
            send_sem=dp_send_sem.at[phase, peer],
            recv_sem=dp_recv_sem.at[phase, mine],
            device_id=(peer, j),
            device_id_type=MESH,
        )

    def loop(count, body, first=0):
        def step(t, carry):
            body(t)
            return carry

        lax.fori_loop(first, count, step, 0)

    for r in range(ring):
        cache_copy(r).start()
    value_copy.start()
    loop(pairs, lambda t: wo_copy(lax.rem(chip + 1 + t, pairs)).start())

    barrier = pltpu.get_barrier_semaphore()

    def greet_tp(d):
        pl.semaphore_signal(
            barrier, inc=1, device_id=(i, lax.rem(j + d, n)), device_id_type=MESH
        )

    def greet_dp(d):
        pl.semaphore_signal(
            barrier, inc=1, device_id=(lax.rem(i + d, m), j), device_id_type=MESH
        )

    loop(n, greet_tp, 1)
    loop(m, greet_dp, 1)

    def score(r):
        cache_copy(r).wait()
        return jnp.dot(query[r], cache_v[r % ring], preferred_element_type=F32) * score_scale

    def attend(r, scores):
        visible = lax.broadcasted_iota(jnp.int32, scores.shape, 1) < lengths[r]
        scores = jnp.where(visible, scores, F32(-1e30))
        peak = jnp.max(scores, axis=1, keepdims=True)
        raised = jnp.where(visible, jnp.exp(scores - peak), F32(0.0))
        total = jnp.sum(raised, axis=1, keepdims=True)
        mixed = lax.dot_general(
            raised.astype(BF16),
            cache_v[r % ring, :width, :],
            (((1,), (1,)), ((), ())),
            preferred_element_type=F32,
        )
        lat[r] = (mixed / total).astype(BF16)

    def send_latents(p):
        found = lat[p * half : (p + 1) * half].reshape(half * heads, width)
        moved = jnp.dot(send_move[...], found, preferred_element_type=F32)
        lat_send[p] = moved.reshape(n, half * each, width).astype(BF16)

        def send_latent(d):
            peer = lax.rem(j + d, n)
            tp_copy(p, lat_send.at[p, peer], lat_recv.at[p, j], peer, j).start()

        loop(n, send_latent, 1)
        lat_recv[p, j] = lat_send[p, j]

    ahead = score(0)
    for r in range(slots):
        scores = ahead
        if r + 1 < slots:
            ahead = score(r + 1)
        attend(r, scores)
        if r + ring < slots:
            cache_copy(r + ring).start()
        if r == 0:
            loop(pairs, lambda b: gate_copy(b).start())
            loop(pairs, lambda b: up_copy(b).start())
        if r == slots - 2:
            for chunk in places:
                down_copy(chunk).start()
        if r == half - 1:
            pl.semaphore_wait(barrier, n - 1 + m - 1)
            send_latents(0)
    send_latents(1)
    value_copy.wait()

    taken = jnp.zeros((each * group, width), F32)
    for p in range(2):

        def wait_latent(d):
            peer = lax.rem(j + n - d, n)
            tp_copy(p, lat_send.at[p, peer], lat_recv.at[p, peer], peer, peer).wait_recv()

        loop(n, wait_latent, 1)
        arrived = lat_recv[p].astype(F32).reshape(n * half * each, width).astype(BF16)
        taken = taken + jnp.dot(take_move[p], arrived, preferred_element_type=F32)
    taken = taken.astype(BF16)
    head = value_v.shape[2]
    for h in range(each):
        flat[:, h * head : (h + 1) * head] = jnp.dot(
            taken[h * group : (h + 1) * group], value_v[h], preferred_element_type=F32
        ).astype(BF16)

    def project(t):
        q = lax.rem(chip + 1 + t, pairs)
        wo_copy(q).wait()
        part = jnp.dot(flat[...], wo_v[q], preferred_element_type=F32)
        mine = layer_input[:, pl.ds(pl.multiple_of(q * wide_cols, 128), wide_cols)].astype(F32)
        row = lax.broadcasted_iota(jnp.int32, part.shape, 0)
        for r in range(slots):
            part = part + jnp.where(row == j * slots + r, mine[r : r + 1, :], F32(0.0))
        for k in range(row_blocks):
            for c in range(2):
                peer = k * blocks + q * 2 + c
                piece = part[k * rows : (k + 1) * rows, c * cols : (c + 1) * cols]

                @pl.when(peer == j)
                def _():
                    rs_own[...] = piece

                @pl.when(peer != j)
                def _():
                    rs_send[peer] = piece.astype(BF16)
                    tp_copy(2, rs_send.at[peer], rs_recv.at[j], peer, j).start()

    loop(pairs, project)

    def add_part(d):
        peer = lax.rem(j + n - d, n)
        tp_copy(2, rs_send.at[peer], rs_recv.at[peer], peer, peer).wait_recv()
        rs_own[...] += rs_recv[peer].astype(F32)

    loop(n, add_part, 1)
    ag[j] = rs_own[...].astype(BF16)

    tp_copy(3, ag.at[j], ag.at[j], sibling, j).start()

    def send_residual(d):
        peer = lax.rem(chip + d, chips) * 2 + core
        tp_copy(3, ag.at[j], ag.at[j], peer, j).start()

    loop(chips, send_residual, 1)
    acc_gate[...] = jnp.zeros_like(acc_gate)
    acc_up[...] = jnp.zeros_like(acc_up)
    square[...] = jnp.zeros_like(square)

    def wait_weights(b):
        gate_copy(b).wait()
        up_copy(b).wait()

    loop(pairs, wait_weights)

    def hand_on(source):
        return pltpu.make_async_remote_copy(
            src_ref=ag.at[source],
            dst_ref=ag.at[source],
            send_sem=send_sem.at[4, source],
            recv_sem=recv_sem.at[3, source],
            device_id=(i, sibling),
            device_id_type=MESH,
        )

    def expand(first, lo, hi, t):
        q = lax.rem(chip + chips - t, chips)
        if first:

            @pl.when(t + 1 < chips)
            def _():
                later = lax.rem(chip + chips - t - 1, chips) * 2 + core
                tp_copy(3, ag.at[later], ag.at[later], later, later).wait_recv()
                hand_on(later).start()

            other = q * 2 + 1 - core
            tp_copy(3, ag.at[other], ag.at[other], sibling, other).wait_recv()
        k = lax.div(q, pairs)
        b = lax.rem(q, pairs)
        wide = jnp.concatenate([ag[q * 2], ag[q * 2 + 1]], axis=1).astype(F32)
        if first:
            square[k] += jnp.sum(wide * wide, axis=1, keepdims=True)
        scaled = (wide * gain[b]).astype(BF16)
        acc_gate[k, :, lo:hi] += jnp.dot(scaled, gate_v[b, :, lo:hi], preferred_element_type=F32)
        acc_up[k, :, lo:hi] += jnp.dot(scaled, up_v[b, :, lo:hi], preferred_element_type=F32)

    for p, (lo, hi) in enumerate(parts):
        loop(chips, functools.partial(expand, p == 0, lo, hi))
        for k in range(row_blocks):
            norm = lax.rsqrt(square[k] * (1.0 / (blocks * cols)) + norm_eps)
            gate = acc_gate[k, :, lo:hi] * norm
            upward = acc_up[k, :, lo:hi] * norm
            inner[p][i, k * rows : (k + 1) * rows, :] = (
                gate / (1.0 + jnp.exp(-gate)) * upward
            ).astype(BF16)

        def send_inner(d):
            peer = lax.rem(i + d, m)
            dp_copy(p, inner[p].at[i], inner[p].at[i], peer, i).start()

        loop(m, send_inner, 1)

    fs_send = rs_send
    share = m * slots

    def drain_parts(d):
        peer = lax.rem(j + d, n)
        tp_copy(2, rs_send.at[peer], rs_recv.at[peer], peer, peer).wait_send()

    for chunk in places:
        down_copy(chunk).wait()
    pieces = blocks // m
    fed = [jnp.zeros((m * group, cols), F32) for _ in range(pieces)]
    for p, (lo, hi) in enumerate(parts):

        def wait_inner(d):
            peer = lax.rem(i + m - d, m)
            dp_copy(p, inner[p].at[peer], inner[p].at[peer], peer, peer).wait_recv()

        loop(m, wait_inner, 1)
        every = inner[p][...].reshape(m * group, hi - lo)
        turned = jnp.dot(turn_move[...], every, preferred_element_type=F32).astype(BF16)
        for c in range(pieces):
            for at, end in chunks[p]:
                fed[c] = fed[c] + jnp.dot(
                    turned[:, at - lo : end - lo],
                    cache_v[places[at, end], : end - at, c * cols : (c + 1) * cols],
                    preferred_element_type=F32,
                )
            if p == len(parts) - 1:
                if c == 0:
                    loop(n, drain_parts, 1)
                fs_send[:, c * share : (c + 1) * share, :] = (
                    fed[c].reshape(n, share, cols).astype(BF16)
                )

                def send_feed(d):
                    peer = lax.rem(j + d, n)
                    tp_copy(5 + c, fs_send.at[peer, pl.ds(c * share, share)], fs_recv.at[c, j], peer, j).start()

                loop(n, send_feed, 1)

    pick_row = lax.broadcasted_iota(jnp.int32, (8, rows), 0)
    pick_col = lax.broadcasted_iota(jnp.int32, (8, rows), 1)
    pick = jnp.where(pick_col == pick_row + jf * slots, F32(1.0), F32(0.0)).astype(BF16)
    live = lax.broadcasted_iota(jnp.int32, (slots, cols), 0) < counts[0]

    lanes = z_send.shape[3]
    for c in range(pieces):

        def add_feed(d, total):
            peer = lax.rem(j + n - d, n)
            tp_copy(5 + c, fs_send.at[peer, pl.ds(c * share, share)], fs_recv.at[c, peer], peer, peer).wait_recv()
            return total + fs_recv[c, peer].astype(F32)

        total = lax.fori_loop(1, n, add_feed, fs_send[j, c * share : (c + 1) * share].astype(F32))
        for g in range(m):
            for e, at in enumerate(range(0, cols, lanes)):
                span = min(lanes, cols - at)
                z_wide[g, e * slots : (e + 1) * slots, :span] = total[
                    g * slots : (g + 1) * slots, at : at + span
                ]
        z_send[c] = z_wide[...].astype(BF16)

        def send_z(d):
            peer = lax.rem(i + d, m)
            dp_copy(2 + c, z_send.at[c, peer], z_recv.at[c, i], peer, i).start()

        loop(m, send_z, 1)
        z_recv[c, i] = z_send[c, i]

    for c in range(pieces):

        def wait_z(d):
            peer = lax.rem(i + m - d, m)
            dp_copy(2 + c, z_send.at[c, peer], z_recv.at[c, peer], peer, peer).wait_recv()

        loop(m, wait_z, 1)
        for g in range(m):
            b = g * pieces + c
            residual = jnp.dot(pick, ag[jr * blocks + b], preferred_element_type=F32)
            summed = z_recv[c, g].astype(F32)
            for e, at in enumerate(range(0, cols, lanes)):
                span = min(lanes, cols - at)
                mixed = residual[:slots, at : at + span] + summed[
                    e * slots : (e + 1) * slots, :span
                ]
                out[:, b * cols + at : b * cols + at + span] = jnp.where(
                    live[:, :span], mixed, F32(0.0)
                ).astype(BF16)

    def drain(d):
        peer = lax.rem(j + d, n)
        for p in range(2):
            tp_copy(p, lat_send.at[p, peer], lat_recv.at[p, peer], peer, peer).wait_send()
        for c in range(pieces):
            tp_copy(5 + c, fs_send.at[peer, pl.ds(c * share, share)], fs_recv.at[c, peer], peer, peer).wait_send()

    def drain_residual(d):
        peer = lax.rem(chip + d, chips) * 2 + core
        tp_copy(3, ag.at[j], ag.at[j], peer, peer).wait_send()
        hand_on(peer).wait_send()

    def drain_dp(d):
        peer = lax.rem(i + d, m)
        for p in range(len(parts)):
            dp_copy(p, inner[p].at[i], inner[p].at[i], peer, peer).wait_send()
        for c in range(pieces):
            dp_copy(2 + c, z_send.at[c, peer], z_recv.at[c, peer], peer, peer).wait_send()

    loop(n, drain, 1)
    tp_copy(3, ag.at[j], ag.at[j], sibling, sibling).wait_send()
    loop(chips, drain_residual, 1)
    loop(m, drain_dp, 1)


def on_device(
    n,
    m,
    layer_input,
    query,
    cache,
    lengths,
    counts,
    value_weight,
    output_weight,
    norm_gain,
    gate_weight,
    up_weight,
    down_weight,
):
    slots, features = layer_input.shape
    heads = query.shape[1]
    each, width, head = value_weight.shape
    hidden = gate_weight.shape[1]
    group = n * slots
    blocks = math.gcd(n, features // 128)
    cols = features // blocks
    rows = group * blocks // n
    pieces = blocks // m
    lanes = (cols // 4 + 127) // 128 * 128
    cache = cache.transpose(0, 2, 1)
    moves = row_moves(n, m, slots, heads)
    vmem = pl.BlockSpec(memory_space=pltpu.VMEM)
    smem = pl.BlockSpec(memory_space=pltpu.SMEM)
    hbm = pl.BlockSpec(memory_space=pl.ANY)
    dma = pltpu.SemaphoreType.DMA
    return pl.pallas_call(
        functools.partial(kernel, n, m, blocks),
        out_shape=jax.ShapeDtypeStruct((slots, features), BF16),
        in_specs=[smem, smem, vmem, vmem, hbm, hbm, hbm, vmem, hbm, hbm, hbm, vmem, vmem, vmem],
        out_specs=vmem,
        scratch_shapes=[
            pltpu.VMEM(cache.shape, BF16),
            pltpu.VMEM(value_weight.shape, BF16),
            pltpu.VMEM((blocks // 2, each * head, 2 * cols), BF16),
            pltpu.VMEM((blocks // 2, 2 * cols, hidden), BF16),
            pltpu.VMEM((blocks // 2, 2 * cols, hidden), BF16),
            pltpu.VMEM((slots, heads, width), BF16),
            pltpu.VMEM((2, n, slots // 2 * each, width), BF16),
            pltpu.VMEM((2, n, slots // 2 * each, width), BF16),
            pltpu.VMEM((group, each * head), BF16),
            pltpu.VMEM((n, rows, cols), BF16),
            pltpu.VMEM((n, rows, cols), BF16),
            pltpu.VMEM((rows, cols), F32),
            pltpu.VMEM((n, rows, cols), BF16),
            pltpu.VMEM((group // rows, rows, hidden), F32),
            pltpu.VMEM((group // rows, rows, hidden), F32),
            pltpu.VMEM((group // rows, rows, 1), F32),
            [pltpu.VMEM((m, group, hi - lo), BF16) for lo, hi in hidden_parts(hidden)],
            pltpu.VMEM((pieces, n, m * slots, cols), BF16),
            pltpu.VMEM((m, 4 * slots, lanes), F32),
            pltpu.VMEM((pieces, m, 4 * slots, lanes), BF16),
            pltpu.VMEM((pieces, m, 4 * slots, lanes), BF16),
            dma((slots,)),
            dma((slots,)),
            dma((blocks // 2,)),
            dma((blocks // 2,)),
            dma((blocks // 2,)),
            dma((5 + pieces, n)),
            dma((5 + pieces, n)),
            dma((2 + pieces, m)),
            dma((2 + pieces, m)),
        ],
        compiler_params=pltpu.CompilerParams(
            collective_id=0, has_side_effects=True, vmem_limit_bytes=64 * 1024 * 1024
        ),
    )(
        lengths,
        counts,
        layer_input,
        query,
        cache,
        value_weight,
        output_weight,
        norm_gain.reshape(blocks // 2, 1, 2 * cols),
        gate_weight,
        up_weight,
        down_weight,
        *[jnp.asarray(x) for x in moves],
    )


def solution(mesh):
    placed = (
        P(("dp", "tp"), None),
        P(("dp", "tp"), None, None),
        P(("dp", "tp"), None, None),
        P(("dp", "tp")),
        P(("dp", "tp")),
        P("tp", None, None),
        P("tp", None),
        P(),
        P(None, "tp"),
        P(None, "tp"),
        P("tp", "dp"),
    )
    return jax.shard_map(
        functools.partial(on_device, mesh.shape["tp"], mesh.shape["dp"]),
        mesh=mesh,
        in_specs=placed,
        out_specs=P(("dp", "tp"), None),
        check_vma=False,
    )
```

time: 75.6 us -> 54.2 us (0.72)
  local copies, waits for them, and re-layouts: 15.6 us -> 1.46 us
  Pallas kernels: 58.8 us -> 51.9 us
    unnamed x2 -> x1, local copies, waits for them, and re-layouts: 15.6 us -> 1.46 us
    pallas_call x1, Pallas kernels: 58.8 us -> 51.9 us  [on_device(): pl.pallas_call(functools.partial(kernel, n, m, blocks), out_shape=jax.Sha...]
where the time goes in v2:
time: 54.2 us; the launch traced here: 54 us
  Pallas kernels  51.9 us (96%)
  local copies, waits for them, and re-layouts  1.46 us (3%)
  between operations  0.66 us (1%)
    pallas_call x1, Pallas kernels, on_device(): pl.pallas_call(functools.partial(kernel, n, m, blocks), out_shape=jax.Sha...  51.9 us
    unnamed x1, local copies, waits for them, and re-layouts  1.46 us

profile of v2, /device:TPU:0, one launch (start us, length us, event | category | flops | bytes accessed | tf_op | source)
XLA Modules:
  0.0 54.0 jit_solution(5154612980634299529)
XLA Ops:
  0.7 51.9 %shard_map.136 = bf16[4,7168]{1,0:T(4,128)(2,1)} custom-call(s32[4]{0:T(128)} %lengths.1, s32[1]{0:T(128)S(6)} %copy.16.counts, bf16[4,7168]{1,0:T(4,128)(2,1)} %layer_input.1, bf16[4,64,576]{2,1,0:T(8,128)(2,1)} %query.1, bf16[4,576,2048]{2,1,0:T(8,128)(2,1)} %bitcast.2, bf16[8,512,128]{2,1,0:T(8,128)(2,1)} %value_weight.1, ...), custom_call_target="tpu_custom_call" | custom-call | tf_op jit(solution)/shard_map/pallas_call | solution.py:505
  52.6 1.5 %copy.17 = bf16[4,7168]{1,0:T(4,128)(2,1)} copy(bf16[4,7168]{1,0:T(4,128)(2,1)} %shard_map.136) | data formatting | bytes 114688

commit v3 on v2

--- a/solution.py
+++ b/solution.py
@@ -37,8 +37,9 @@
 def hidden_parts(hidden):
     if hidden % 128 or hidden < 512:
         return ((0, hidden),)
-    first = (hidden // 2 + 127) // 128 * 128
-    return ((0, first), (first, hidden))
+    first = hidden * 4 // 9 // 128 * 128
+    second = first + hidden // 3 // 128 * 128
+    return ((0, first), (first, second), (second, hidden))
 
 
 def hidden_chunks(hidden):
@@ -83,6 +84,7 @@
     acc_up,
     square,
     inner,
+    rs_pair,
     fs_recv,
     z_wide,
     z_send,
@@ -174,10 +176,11 @@
 
         lax.fori_loop(first, count, step, 0)
 
-    for r in range(ring):
-        cache_copy(r).start()
-    value_copy.start()
-    loop(pairs, lambda t: wo_copy(lax.rem(chip + 1 + t, pairs)).start())
+    def start_wo(t):
+        wo_copy(lax.rem(chip + 1 + t, pairs)).start()
+
+    cache_copy(0).start()
+    cache_copy(1).start()
 
     barrier = pltpu.get_barrier_semaphore()
 
@@ -196,6 +199,11 @@
 
     def score(r):
         cache_copy(r).wait()
+        if r == 0:
+            for later in range(2, slots):
+                cache_copy(later).start()
+            value_copy.start()
+            start_wo(0)
         return jnp.dot(query[r], cache_v[r % ring], preferred_element_type=F32) * score_scale
 
     def attend(r, scores):
@@ -224,18 +232,23 @@
         loop(n, send_latent, 1)
         lat_recv[p, j] = lat_send[p, j]
 
+    def start_weights(t):
+        b = lax.rem(chip + chips - t, pairs)
+        gate_copy(b).start()
+        up_copy(b).start()
+
     ahead = score(0)
     for r in range(slots):
         scores = ahead
         if r + 1 < slots:
             ahead = score(r + 1)
         attend(r, scores)
-        if r + ring < slots:
-            cache_copy(r + ring).start()
         if r == 0:
-            loop(pairs, lambda b: gate_copy(b).start())
-            loop(pairs, lambda b: up_copy(b).start())
+            loop(pairs, start_wo, 1)
+        if r == 1:
+            start_weights(0)
         if r == slots - 2:
+            loop(pairs, start_weights, 1)
             for chunk in places:
                 down_copy(chunk).start()
         if r == half - 1:
@@ -304,12 +317,6 @@
     acc_up[...] = jnp.zeros_like(acc_up)
     square[...] = jnp.zeros_like(square)
 
-    def wait_weights(b):
-        gate_copy(b).wait()
-        up_copy(b).wait()
-
-    loop(pairs, wait_weights)
-
     def hand_on(source):
         return pltpu.make_async_remote_copy(
             src_ref=ag.at[source],
@@ -334,15 +341,30 @@
             tp_copy(3, ag.at[other], ag.at[other], sibling, other).wait_recv()
         k = lax.div(q, pairs)
         b = lax.rem(q, pairs)
-        wide = jnp.concatenate([ag[q * 2], ag[q * 2 + 1]], axis=1).astype(F32)
         if first:
+
+            @pl.when(t < pairs)
+            def _():
+                gate_copy(b).wait()
+                up_copy(b).wait()
+
+        if first:
+            wide = jnp.concatenate([ag[q * 2], ag[q * 2 + 1]], axis=1).astype(F32)
             square[k] += jnp.sum(wide * wide, axis=1, keepdims=True)
-        scaled = (wide * gain[b]).astype(BF16)
+            scaled = (wide * gain[b]).astype(BF16)
+            rs_recv[q * 2] = scaled[:, :cols]
+            rs_recv[q * 2 + 1] = scaled[:, cols:]
+        else:
+            scaled = jnp.concatenate([rs_recv[q * 2], rs_recv[q * 2 + 1]], axis=1)
         acc_gate[k, :, lo:hi] += jnp.dot(scaled, gate_v[b, :, lo:hi], preferred_element_type=F32)
         acc_up[k, :, lo:hi] += jnp.dot(scaled, up_v[b, :, lo:hi], preferred_element_type=F32)
 
     for p, (lo, hi) in enumerate(parts):
-        loop(chips, functools.partial(expand, p == 0, lo, hi))
+        if p > 0 and chips <= 4:
+            for t in range(chips):
+                expand(False, lo, hi, t)
+        else:
+            loop(chips, functools.partial(expand, p == 0, lo, hi))
         for k in range(row_blocks):
             norm = lax.rsqrt(square[k] * (1.0 / (blocks * cols)) + norm_eps)
             gate = acc_gate[k, :, lo:hi] * norm
@@ -359,6 +381,24 @@
 
     fs_send = rs_send
     share = m * slots
+
+    def piece_of(c):
+        return pl.ds(c * share, share)
+
+    def pair_copy(c, q):
+        return pltpu.make_async_remote_copy(
+            src_ref=fs_send.at[q * 2 + 1 - core, piece_of(c)],
+            dst_ref=rs_pair.at[q, piece_of(c)],
+            send_sem=send_sem.at[5 + c, q],
+            recv_sem=recv_sem.at[5 + c, q],
+            device_id=(i, sibling),
+            device_id_type=MESH,
+        )
+
+    def feed_copy(c, peer, origin):
+        return tp_copy(
+            5 + pieces + c, fs_send.at[peer, piece_of(c)], fs_recv.at[c, origin], peer, origin
+        )
 
     def drain_parts(d):
         peer = lax.rem(j + d, n)
@@ -391,11 +431,25 @@
                     fed[c].reshape(n, share, cols).astype(BF16)
                 )
 
-                def send_feed(d):
-                    peer = lax.rem(j + d, n)
-                    tp_copy(5 + c, fs_send.at[peer, pl.ds(c * share, share)], fs_recv.at[c, j], peer, j).start()
-
-                loop(n, send_feed, 1)
+                def send_pair(d):
+                    q = lax.rem(chip + d, chips)
+                    pair_copy(c, q).start()
+
+                loop(chips + 1, send_pair, 1)
+
+    for c in range(pieces):
+
+        def send_feed(d):
+            q = lax.rem(chip + d, chips)
+            peer = q * 2 + core
+            pair_copy(c, q).wait_recv()
+            summed = fs_send[peer, c * share : (c + 1) * share].astype(F32) + rs_pair[
+                q, c * share : (c + 1) * share
+            ].astype(F32)
+            fs_send[peer, c * share : (c + 1) * share] = summed.astype(BF16)
+            feed_copy(c, peer, chip).start()
+
+        loop(chips, send_feed, 1)
 
     pick_row = lax.broadcasted_iota(jnp.int32, (8, rows), 0)
     pick_col = lax.broadcasted_iota(jnp.int32, (8, rows), 1)
@@ -406,11 +460,15 @@
     for c in range(pieces):
 
         def add_feed(d, total):
-            peer = lax.rem(j + n - d, n)
-            tp_copy(5 + c, fs_send.at[peer, pl.ds(c * share, share)], fs_recv.at[c, peer], peer, peer).wait_recv()
-            return total + fs_recv[c, peer].astype(F32)
-
-        total = lax.fori_loop(1, n, add_feed, fs_send[j, c * share : (c + 1) * share].astype(F32))
+            q = lax.rem(chip + chips - d, chips)
+            feed_copy(c, q * 2 + core, q).wait_recv()
+            return total + fs_recv[c, q].astype(F32)
+
+        pair_copy(c, chip).wait_recv()
+        total = fs_send[j, c * share : (c + 1) * share].astype(F32) + rs_pair[
+            chip, c * share : (c + 1) * share
+        ].astype(F32)
+        total = lax.fori_loop(1, chips, add_feed, total)
         for g in range(m):
             for e, at in enumerate(range(0, cols, lanes)):
                 span = min(lanes, cols - at)
@@ -421,7 +479,7 @@
 
         def send_z(d):
             peer = lax.rem(i + d, m)
-            dp_copy(2 + c, z_send.at[c, peer], z_recv.at[c, i], peer, i).start()
+            dp_copy(len(parts) + c, z_send.at[c, peer], z_recv.at[c, i], peer, i).start()
 
         loop(m, send_z, 1)
         z_recv[c, i] = z_send[c, i]
@@ -430,7 +488,7 @@
 
         def wait_z(d):
             peer = lax.rem(i + m - d, m)
-            dp_copy(2 + c, z_send.at[c, peer], z_recv.at[c, peer], peer, peer).wait_recv()
+            dp_copy(len(parts) + c, z_send.at[c, peer], z_recv.at[c, peer], peer, peer).wait_recv()
 
         loop(m, wait_z, 1)
         for g in range(m):
@@ -450,24 +508,29 @@
         peer = lax.rem(j + d, n)
         for p in range(2):
             tp_copy(p, lat_send.at[p, peer], lat_recv.at[p, peer], peer, peer).wait_send()
-        for c in range(pieces):
-            tp_copy(5 + c, fs_send.at[peer, pl.ds(c * share, share)], fs_recv.at[c, peer], peer, peer).wait_send()
 
     def drain_residual(d):
         peer = lax.rem(chip + d, chips) * 2 + core
         tp_copy(3, ag.at[j], ag.at[j], peer, peer).wait_send()
         hand_on(peer).wait_send()
+        for c in range(pieces):
+            feed_copy(c, peer, chip).wait_send()
+
+    def drain_pair(q):
+        for c in range(pieces):
+            pair_copy(c, q).wait_send()
 
     def drain_dp(d):
         peer = lax.rem(i + d, m)
         for p in range(len(parts)):
             dp_copy(p, inner[p].at[i], inner[p].at[i], peer, peer).wait_send()
         for c in range(pieces):
-            dp_copy(2 + c, z_send.at[c, peer], z_recv.at[c, peer], peer, peer).wait_send()
+            dp_copy(len(parts) + c, z_send.at[c, peer], z_recv.at[c, peer], peer, peer).wait_send()
 
     loop(n, drain, 1)
     tp_copy(3, ag.at[j], ag.at[j], sibling, sibling).wait_send()
     loop(chips, drain_residual, 1)
+    loop(chips, drain_pair)
     loop(m, drain_dp, 1)
 
 
@@ -525,7 +588,8 @@
             pltpu.VMEM((group // rows, rows, hidden), F32),
             pltpu.VMEM((group // rows, rows, 1), F32),
             [pltpu.VMEM((m, group, hi - lo), BF16) for lo, hi in hidden_parts(hidden)],
-            pltpu.VMEM((pieces, n, m * slots, cols), BF16),
+            pltpu.VMEM((n // 2, pieces * m * slots, cols), BF16),
+            pltpu.VMEM((pieces, n // 2, m * slots, cols), BF16),
             pltpu.VMEM((m, 4 * slots, lanes), F32),
             pltpu.VMEM((pieces, m, 4 * slots, lanes), BF16),
             pltpu.VMEM((pieces, m, 4 * slots, lanes), BF16),
@@ -534,10 +598,10 @@
             dma((blocks // 2,)),
             dma((blocks // 2,)),
             dma((blocks // 2,)),
-            dma((5 + pieces, n)),
-            dma((5 + pieces, n)),
-            dma((2 + pieces, m)),
-            dma((2 + pieces, m)),
+            dma((5 + 2 * pieces, n)),
+            dma((5 + 2 * pieces, n)),
+            dma((len(hidden_parts(hidden)) + pieces, m)),
+            dma((len(hidden_parts(hidden)) + pieces, m)),
         ],
         compiler_params=pltpu.CompilerParams(
             collective_id=0, has_side_effects=True, vmem_limit_bytes=64 * 1024 * 1024

time: 54.2 us -> 53.8 us (level)
  no operation moved by 1% of the time
where the time goes in v3:
time: 53.8 us; the launch traced here: 53.6 us
  Pallas kernels  51.5 us (96%)
  local copies, waits for them, and re-layouts  1.46 us (3%)
  between operations  0.66 us (1%)
    pallas_call x1, Pallas kernels, on_device(): pl.pallas_call(functools.partial(kernel, n, m, blocks), out_shape=jax.Sha...  51.5 us
    unnamed x1, local copies, waits for them, and re-layouts  1.46 us

profile of v3, /device:TPU:0, one launch (start us, length us, event | category | flops | bytes accessed | tf_op | source)
XLA Modules:
  0.0 53.6 jit_solution(9321103631936206708)
XLA Ops:
  0.7 51.5 %shard_map.136 = bf16[4,7168]{1,0:T(4,128)(2,1)} custom-call(s32[4]{0:T(128)} %lengths.1, s32[1]{0:T(128)S(6)} %copy.16.counts, bf16[4,7168]{1,0:T(4,128)(2,1)} %layer_input.1, bf16[4,64,576]{2,1,0:T(8,128)(2,1)} %query.1, bf16[4,576,2048]{2,1,0:T(8,128)(2,1)} %bitcast.2, bf16[8,512,128]{2,1,0:T(8,128)(2,1)} %value_weight.1, ...), custom_call_target="tpu_custom_call" | custom-call | tf_op jit(solution)/shard_map/pallas_call | solution.py:568
  52.1 1.5 %copy.17 = bf16[4,7168]{1,0:T(4,128)(2,1)} copy(bf16[4,7168]{1,0:T(4,128)(2,1)} %shard_map.136) | data formatting | bytes 114688
